TPU v7x, 32 devices: a whole 2x2x4 slice. The times are simulated.
32 devices in a mesh: tm: 4 (over z), sx: 2 (over y), sy: 4 (over x, core).
Axes of the slice: x: 2, y: 2, z: 4, core: 2. Of those that a mesh axis runs over, the one named last changes fastest.
Arguments:
- wall_temp: bfloat16 [64, 8192, 128], P('tm', ('sx', 'sy')), may hold values from -6 to 6
- owner_map: int32 [8192, 1], P(('sx', 'sy')), may hold values from 0 to 7; in each aligned block of 1024 rows (0 to 1023, 1024 to 2047, ...) at most 256 rows name the same one
- stencil_column: int32 [8192], P(('sx', 'sy')), may hold values from 0 to 255
- material: int32 [32, 64, 128], P('sx', 'sy'), may hold values from 0 to 3
- conductivity: float32 [4], replicated, may hold values from 0.1 to 1
- capacity: float32 [4], replicated, may hold values from 0.2 to 1
Outputs:
- temperature: float32 [32, 2, 32, 64, 128], P('tm', None, 'sx', 'sy')
Inputs may be any that keep to these rules, and one draw needn't show every extreme that they name: `owner_map`: among the 1024 patches of one device (aligned blocks of rows), no owner is named more than 256 times, a bound that some block reaches.
All inputs are finite; a program needn't handle non-finite values.
Results may differ from a plain program's by a relative error of at most 0.0034.
Values may be sent and summed in bfloat16 or wider, within the bound.
A program may use at most 64 MiB of HBM per device.

v0:
```python
import math

import jax
import jax.numpy as jnp
from jax import lax
from jax.sharding import PartitionSpec as P

TIME = 64
HARM = 32
NMAT = 4
SWEEPS = 4


omega_step = 0.1


def with_halo(block, sides, width):
    for axis, dim in sides:
        count = lax.axis_size(axis)
        forward = [(i, i + 1) for i in range(count - 1)]
        backward = [(target, source) for source, target in forward]
        low = lax.ppermute(
            lax.slice_in_dim(block, block.shape[dim] - width, None, axis=dim), axis, forward
        )
        high = lax.ppermute(lax.slice_in_dim(block, 0, width, axis=dim), axis, backward)
        block = jnp.concatenate([low, block, high], axis=dim)
    return block


def dft_table():
    freq_index = jnp.arange(HARM, dtype=jnp.int32)
    time_index = jnp.arange(TIME, dtype=jnp.int32)
    phase_int = freq_index[:, None] * time_index[None, :] % TIME
    angles = phase_int.astype(jnp.float32) * jnp.float32(2.0 * math.pi / TIME)
    amplitude = jnp.float32(2.0 / math.sqrt(TIME))
    table_rows = jnp.stack([amplitude * jnp.cos(angles), -amplitude * jnp.sin(angles)], axis=1)
    return table_rows.reshape(2 * HARM, TIME).astype(jnp.bfloat16)


def lookup(material, table):
    values = jnp.zeros(material.shape, jnp.float32)
    for material_id in range(NMAT):
        values = jnp.where(material == material_id, table[material_id], values)
    return values


def face_value(conduct, other):
    other = jnp.where(other > 0, other, conduct)
    return 2.0 * conduct * other / (conduct + other)


def face_values(conduct, padded):
    next_x = face_value(conduct, padded[2:, 1:-1, 1:-1])
    prev_x = face_value(conduct, padded[:-2, 1:-1, 1:-1])
    next_y = face_value(conduct, padded[1:-1, 2:, 1:-1])
    prev_y = face_value(conduct, padded[1:-1, :-2, 1:-1])
    next_z = face_value(conduct, padded[1:-1, 1:-1, 2:])
    prev_z = face_value(conduct, padded[1:-1, 1:-1, :-2])
    total = next_x + prev_x + next_y + prev_y + next_z + prev_z
    return ((next_x, prev_x, next_y, prev_y, next_z, prev_z), total)


def relax_sweep(padded, source, faces, real_den, imag_den):
    next_x, prev_x, next_y, prev_y, next_z, prev_z = faces
    nearby = next_x * padded[..., 2:, 1:-1, 1:-1] + prev_x * padded[..., :-2, 1:-1, 1:-1]
    nearby = nearby + next_y * padded[..., 1:-1, 2:, 1:-1] + prev_y * padded[..., 1:-1, :-2, 1:-1]
    nearby = nearby + next_z * padded[..., 1:-1, 1:-1, 2:] + prev_z * padded[..., 1:-1, 1:-1, :-2]
    numerator = source + nearby
    real_num = numerator[..., 0, :, :, :]
    imag_num = numerator[..., 1, :, :, :]
    modulus = real_den * real_den + imag_den * imag_den
    real_out = (real_num * real_den + imag_num * imag_den) / modulus
    imag_out = (imag_num * real_den - real_num * imag_den) / modulus
    return jnp.stack([real_out, imag_out], axis=-4)


def to_harmonics(payload):
    transform_rows = dft_table()
    gathered = lax.all_to_all(payload, "tm", split_axis=1, concat_axis=0, tiled=True)
    flattened = gathered.reshape(TIME, gathered.shape[1] * gathered.shape[2])
    harmonic = jnp.dot(transform_rows, flattened, preferred_element_type=jnp.float32)
    harmonic = harmonic.astype(jnp.bfloat16).reshape(2 * HARM, gathered.shape[1], gathered.shape[2])
    return lax.all_to_all(harmonic, "tm", split_axis=0, concat_axis=1, tiled=True)


def to_owners(payload, owner_map, stencil_column):
    owners = lax.axis_size("sx") * lax.axis_size("sy")
    capacity_slots = 2 * payload.shape[1] // owners
    owner_ids = owner_map[:, 0]
    onehot = (owner_ids[:, None] == jnp.arange(owners, dtype=jnp.int32)[None, :]).astype(jnp.int32)
    rank_all = jnp.cumsum(onehot, axis=0) - onehot
    rank_own = jnp.sum(rank_all * onehot, axis=1)
    slot_index = owner_ids * capacity_slots + rank_own
    buffer = jnp.zeros((payload.shape[0], owners * capacity_slots, payload.shape[2]), jnp.bfloat16)
    buffer = buffer.at[:, slot_index, :].set(payload)
    columns = (
        jnp.full((1, owners * capacity_slots), -1, jnp.int32).at[0, slot_index].set(stencil_column)
    )
    return (
        lax.all_to_all(buffer, ("sx", "sy"), split_axis=1, concat_axis=1, tiled=True),
        lax.all_to_all(columns, ("sx", "sy"), split_axis=1, concat_axis=1, tiled=True),
    )


def body(wall_temp, owner_map, stencil_column, material, conductivity, capacity):
    received, columns = to_owners(wall_temp, owner_map, stencil_column)
    harmonic = to_harmonics(received)
    size_x, size_y, size_z = material.shape
    local_harms = harmonic.shape[0] // 2
    column_hits = (jnp.arange(size_x * size_y, dtype=jnp.int32)[:, None] == columns).astype(
        jnp.bfloat16
    )
    source = jnp.einsum("ps,csz->cpz", column_hits, harmonic, preferred_element_type=jnp.float32)
    source = source.reshape(local_harms, 2, size_x, size_y, size_z)
    conduct = lookup(material, conductivity)
    heat_cap = lookup(material, capacity)
    rim = with_halo(conduct.astype(jnp.bfloat16), (("sx", 0), ("sy", 1)), 1).astype(conduct.dtype)
    rim = jnp.pad(rim, ((0, 0), (0, 0), (1, 1)), mode="edge")
    faces, real_den = face_values(conduct, rim)
    harm_index = lax.axis_index("tm") * local_harms + jnp.arange(local_harms, dtype=jnp.int32)
    imag_den = omega_step * harm_index.astype(jnp.float32)[:, None, None, None] * heat_cap
    start = jnp.zeros((local_harms, 2, size_x + 2, size_y + 2, size_z + 2), jnp.float32)
    field = relax_sweep(start, source, faces, real_den, imag_den)
    for sweep in range(SWEEPS - 1):
        padded = with_halo(field, (("sx", 2), ("sy", 3)), 1)
        padded = jnp.pad(padded, ((0, 0), (0, 0), (0, 0), (0, 0), (1, 1)))
        field = relax_sweep(padded, source, faces, real_den, imag_den)
    return field


def solution(mesh):
    in_specs = (
        P("tm", ("sx", "sy"), None),
        P(("sx", "sy"), None),
        P(("sx", "sy")),
        P("sx", "sy", None),
        P(),
        P(),
    )
    out_specs = P("tm", None, "sx", "sy", None)
    return jax.shard_map(body, mesh=mesh, in_specs=in_specs, out_specs=out_specs, check_vma=False)
```

profile of v0, /device:TPU:1, one launch (start us, length us, event | category | flops | bytes accessed | tf_op | source)
XLA Modules:
  0.0 754.0 jit_solution(16703493277641040546)
XLA Ops:
  4.9 6.9 copy.26
  11.8 3.9 broadcast_in_dim.29
  15.7 104.3 %scatter_fusion = bf16[16,2048,128]{2,0,1:T(8,128)(2,1)} fusion(bf16[16,2048,128]{2,0,1:T(8,128)(2,1)} %broadcast_in_dim.29, s32[1024]{0:T(1024)S(1)} %bitcast.70, bf16[1024,16,128]{2,1,0:T(8,128)(2,1)} %copy.26), kind=kCustom, calls=%fused_computation | custom fusion | bytes 12587008 | tf_op jit(solution)/shard_map/scatter | solution.py:95
  120.0 99.1 %all_to_all.47 = bf16[16,2048,128]{2,0,1:T(8,128)(2,1)} all-to-all(bf16[16,2048,128]{2,0,1:T(8,128)(2,1)} %scatter_fusion), channel_id=1, replica_groups=mesh['tm'=4,'sx'=2,'sy'=4] {'sx','sy'}, dimensions={1} | all-to-all | bytes 16777216 | tf_op jit(solution)/shard_map/all_to_all | solution.py:100
  219.1 5.8 all-to-all-start.1
  225.1 183.1 %all-to-all-done.1 = bf16[16,2048,128]{2,0,1:T(8,128)(2,1)} async-done(((bf16[16,2048,128]{2,0,1:T(8,128)(2,1)}), bf16[16,2048,128]{2,0,1:T(8,128)(2,1)}, u32[]{:S(2)}, u32[]{:S(2)}) %all-to-all-start.1) | async-done | bytes 8388640 | tf_op jit(solution)/shard_map/all_to_all | solution.py:79
  408.2 8.8 %copy.27 = bf16[16,4,512,128]{3,2,0,1:T(8,128)(2,1)} copy(bf16[16,4,512,128]{3,0,2,1:T(8,128)(2,1)} %bitcast.7) | data formatting | bytes 16777216 | tf_op jit(solution)/shard_map/all_to_all | solution.py:79
  417.0 13.1 %fusion.3 = bf16[8,8,512,128]{3,1,2,0:T(8,128)(2,1)} fusion(bf16[64,64]{1,0:T(8,128)(2,1)S(1)} %bitcast.69, bf16[8,8,512,128]{3,2,1,0:T(8,128)(2,1)} %bitcast.65), kind=kOutput, calls=%fused_computation.23 | convolution fusion | flops 541065216 | bytes 16785408 | tf_op jit(solution)/shard_map/dot_general | solution.py:81
  430.2 8.9 %copy.32 = bf16[8,8,512,128]{3,2,1,0:T(8,128)(2,1)} copy(bf16[8,8,512,128]{3,1,2,0:T(8,128)(2,1)} %fusion.3) | data formatting | bytes 16777216
  439.1 5.8 all-to-all-start.2
  452.6 4.0 collective-permute-start
  457.4 4.6 collective-permute-start.3
  464.9 5.0 scatter_custom_fusion.1
  470.1 2.8 fusion.74
  473.0 154.6 %all-to-all-done.2 = bf16[64,512,128]{2,1,0:T(8,128)(2,1)} async-done(((bf16[64,512,128]{2,1,0:T(8,128)(2,1)}), bf16[64,512,128]{2,1,0:T(8,128)(2,1)}, u32[]{:S(2)}, u32[]{:S(2)}) %all-to-all-start.2) | async-done | bytes 8388640 | tf_op jit(solution)/shard_map/all_to_all | solution.py:83
  627.5 4.7 all-to-all-start.3
  632.2 14.6 %copy.28 = bf16[4,16,512,128]{2,0,3,1:T(4,128)(2,1)} copy(bf16[4,16,512,128]{3,2,1,0:T(8,128)(2,1)} %bitcast.9) | data formatting | bytes 16777216 | tf_op jit(solution)/shard_map/all_to_all | solution.py:83
  646.8 14.3 %all_to_all.40 = bf16[16,2048,128]{1,2,0:T(8,128)(2,1)} reshape(bf16[16,4,512,128]{2,1,3,0:T(4,128)(2,1)} %bitcast.67) | data formatting | bytes 16777216 | tf_op jit(solution)/shard_map/all_to_all | solution.py:83
  661.2 7.1 fusion.39
  672.3 4.0 collective-permute-start.5
  678.7 3.4 collective-permute-start.6
  682.1 3.2 collective-permute-start.7
  687.4 5.3 select_maximum_fusion.10
  692.7 3.5 fusion.27
  698.0 4.1 collective-permute-start.9
  706.3 5.5 collective-permute-start.11
  713.7 5.3 select_maximum_fusion.5
  719.0 3.5 fusion.17
  724.3 4.1 collective-permute-start.13
  733.2 5.4 collective-permute-start.15
  741.1 6.4 select_maximum_fusion
  747.6 4.6 fusion.7
  (110 shorter events, 43.3 us)
Async XLA Ops:
  219.1 189.1 %all-to-all-start.1 = ((bf16[16,2048,128]{2,0,1:T(8,128)(2,1)}), bf16[16,2048,128]{2,0,1:T(8,128)(2,1)}, u32[]{:S(2)}, u32[]{:S(2)}) async-start(bf16[16,2048,128]{2,0,1:T(8,128)(2,1)} %all_to_all.47), calls=%async_computation.1 | async-start | bytes 16777216 | tf_op jit(solution)/shard_map/all_to_all | solution.py:79
  439.1 17.5 %copy-start.22 = (s32[2]{0:T(128)S(1)}, s32[2]{0:T(128)}, u32[]{:S(2)}) copy-start(s32[2]{0:T(128)} %constant.69) | copy-start | bytes 28
  439.1 17.6 %copy-start.21 = (s32[2]{0:T(128)S(1)}, s32[2]{0:T(128)}, u32[]{:S(2)}) copy-start(s32[2]{0:T(128)} %constant.66) | copy-start | bytes 28
  439.1 188.4 %all-to-all-start.2 = ((bf16[64,512,128]{2,1,0:T(8,128)(2,1)}), bf16[64,512,128]{2,1,0:T(8,128)(2,1)}, u32[]{:S(2)}, u32[]{:S(2)}) async-start(bf16[64,512,128]{2,1,0:T(8,128)(2,1)} %bitcast.66), calls=%async_computation.2 | async-start | bytes 16777216 | tf_op jit(solution)/shard_map/all_to_all | solution.py:83
  451.3 5.5 collective-permute-start.1
  452.6 4.7 collective-permute-start
  457.4 12.5 %collective-permute-start.3 = (bf16[18,1,128]{2,1,0:T(2,128)(2,1)S(1)}, bf16[18,1,128]{2,1,0:T(2,128)(2,1)S(1)}, u32[]{:S(2)}, u32[]{:S(2)}) collective-permute-start(bf16[18,1,128]{2,1,0:T(2,128)(2,1)S(1)} %get-tuple-element.41), channel_id=1, source_target_pairs={{1,0},{2,1},{3,2},{5,4},{6,5},{7,6},{9,8},{10,9},{11,10},{13,12},{... | collective-permute-start | bytes 13832 | tf_op jit(solution)/shard_map/ppermute | solution.py:25
  462.0 7.9 %collective-permute-start.2 = (bf16[18,1,128]{2,1,0:T(2,128)(2,1)S(1)}, bf16[18,1,128]{2,1,0:T(2,128)(2,1)S(1)}, u32[]{:S(2)}, u32[]{:S(2)}) collective-permute-start(bf16[18,1,128]{2,1,0:T(2,128)(2,1)S(1)} %get-tuple-element.40), channel_id=1, source_target_pairs={{0,1},{1,2},{2,3},{4,5},{5,6},{6,7},{8,9},{9,10},{10,11},{12,13},{... | collective-permute-start | bytes 13832 | tf_op jit(solution)/shard_map/ppermute | solution.py:22
  472.9 246.1 %copy-start.2 = (f32[16,16,128]{2,1,0:T(8,128)}, f32[16,16,128]{2,1,0:T(8,128)S(1)}, u32[]{:S(2)}) copy-start(f32[16,16,128]{2,1,0:T(8,128)S(1)} %get-tuple-element.12) | copy-start | bytes 393220
  472.9 246.1 %copy-start.4 = (f32[16,16,128]{2,1,0:T(8,128)}, f32[16,16,128]{2,1,0:T(8,128)S(1)}, u32[]{:S(2)}) copy-start(f32[16,16,128]{2,1,0:T(8,128)S(1)} %get-tuple-element.13) | copy-start | bytes 393220
  472.9 246.1 %copy-start.6 = (f32[16,16,128]{2,1,0:T(8,128)}, f32[16,16,128]{2,1,0:T(8,128)S(1)}, u32[]{:S(2)}) copy-start(f32[16,16,128]{2,1,0:T(8,128)S(1)} %get-tuple-element.14) | copy-start | bytes 393220
  472.9 246.1 %copy-start.8 = (f32[16,16,128]{2,1,0:T(8,128)}, f32[16,16,128]{2,1,0:T(8,128)S(1)}, u32[]{:S(2)}) copy-start(f32[16,16,128]{2,1,0:T(8,128)S(1)} %get-tuple-element.15) | copy-start | bytes 393220
  472.9 246.1 %copy-start.10 = (f32[16,16,128]{2,1,0:T(8,128)}, f32[16,16,128]{2,1,0:T(8,128)S(1)}, u32[]{:S(2)}) copy-start(f32[16,16,128]{2,1,0:T(8,128)S(1)} %get-tuple-element.16) | copy-start | bytes 393220
  473.0 246.1 %copy-start.12 = (f32[16,16,128]{2,1,0:T(8,128)}, f32[16,16,128]{2,1,0:T(8,128)S(1)}, u32[]{:S(2)}) copy-start(f32[16,16,128]{2,1,0:T(8,128)S(1)} %get-tuple-element.17) | copy-start | bytes 393220
  627.5 33.6 %all-to-all-start.3 = ((s32[1,8,256]{2,0,1:T(1,128)}), s32[1,8,256]{2,0,1:T(1,128)S(1)}, u32[]{:S(2)}, u32[]{:S(2)}) async-start(s32[1,8,256]{2,0,1:T(1,128)} %bitcast.11), calls=%async_computation.3 | async-start | bytes 16384 | tf_op jit(solution)/shard_map/all_to_all | solution.py:101
  671.0 6.6 collective-permute-start.4
  672.3 6.2 collective-permute-start.5
  678.7 7.5 collective-permute-start.6
  682.1 5.3 collective-permute-start.7
  696.7 5.8 collective-permute-start.8
  698.0 6.2 collective-permute-start.9
  704.4 8.1 %collective-permute-start.10 = (f32[8,2,18,1,128]{4,3,2,1,0:T(1,128)S(1)}, f32[8,2,18,1,128]{4,3,2,1,0:T(1,128)S(1)}, u32[]{:S(2)}, u32[]{:S(2)}) collective-permute-start(f32[8,2,18,1,128]{4,3,2,1,0:T(1,128)S(1)} %get-tuple-element.29), channel_id=1, source_target_pairs={{1,0},{2,1},{3,2},{5,4},{6,5},{7,6},{9,8},{10,9},{11,10},{13,12},{... | collective-permute-start | bytes 442376 | tf_op jit(solution)/shard_map/ppermute | solution.py:25
  706.3 7.4 collective-permute-start.11
  723.0 5.8 collective-permute-start.12
  724.3 6.0 collective-permute-start.13
  731.3 8.5 %collective-permute-start.14 = (f32[8,2,18,1,128]{4,3,2,1,0:T(1,128)}, f32[8,2,18,1,128]{4,3,2,1,0:T(1,128)}, u32[]{:S(2)}, u32[]{:S(2)}) collective-permute-start(f32[8,2,18,1,128]{4,3,2,1,0:T(1,128)} %get-tuple-element.27), channel_id=1, source_target_pairs={{1,0},{2,1},{3,2},{5,4},{6,5},{7,6},{9,8},{10,9},{11,10},{13,12},{... | collective-permute-start | bytes 442376 | tf_op jit(solution)/shard_map/ppermute | solution.py:25
  733.2 7.8 %collective-permute-start.15 = (f32[8,2,18,1,128]{4,3,2,1,0:T(1,128)}, f32[8,2,18,1,128]{4,3,2,1,0:T(1,128)}, u32[]{:S(2)}, u32[]{:S(2)}) collective-permute-start(f32[8,2,18,1,128]{4,3,2,1,0:T(1,128)} %get-tuple-element.26), channel_id=1, source_target_pairs={{0,1},{1,2},{2,3},{4,5},{5,6},{6,7},{8,9},{9,10},{10,11},{12,13},{... | collective-permute-start | bytes 442376 | tf_op jit(solution)/shard_map/ppermute | solution.py:22
  738.7 8.8 %copy-start.1 = (f32[8,1,16,16,128]{4,3,2,1,0:T(8,128)S(1)}, f32[8,1,16,16,128]{4,3,2,1,0:T(8,128)}, u32[]{:S(2)}) copy-start(f32[8,1,16,16,128]{4,3,2,1,0:T(8,128)} %copy-done) | copy-start | bytes 3145732
  738.7 8.8 %copy-start.3 = (f32[16,16,128]{2,1,0:T(8,128)S(1)}, f32[16,16,128]{2,1,0:T(8,128)}, u32[]{:S(2)}) copy-start(f32[16,16,128]{2,1,0:T(8,128)} %copy-done.2) | copy-start | bytes 393220
  738.7 8.8 %copy-start.5 = (f32[16,16,128]{2,1,0:T(8,128)S(1)}, f32[16,16,128]{2,1,0:T(8,128)}, u32[]{:S(2)}) copy-start(f32[16,16,128]{2,1,0:T(8,128)} %copy-done.4) | copy-start | bytes 393220
  738.7 8.8 %copy-start.7 = (f32[16,16,128]{2,1,0:T(8,128)S(1)}, f32[16,16,128]{2,1,0:T(8,128)}, u32[]{:S(2)}) copy-start(f32[16,16,128]{2,1,0:T(8,128)} %copy-done.6) | copy-start | bytes 393220
  738.7 8.8 %copy-start.9 = (f32[16,16,128]{2,1,0:T(8,128)S(1)}, f32[16,16,128]{2,1,0:T(8,128)}, u32[]{:S(2)}) copy-start(f32[16,16,128]{2,1,0:T(8,128)} %copy-done.8) | copy-start | bytes 393220
  (12 other events, 74.2 us)
where the time goes:
time: 760 us; the launch traced here: 754 us
  waiting for transfers between devices  351 us (46%)
  local copies, waits for them, and re-layouts  172 us (23%)
  blocking collectives  99.1 us (13%)
  starting transfers between devices  66.5 us (9%)
  other arithmetic  45 us (6%)
  matrix products  20.2 us (3%)
    all_to_all x1, waiting for transfers between devices, to_harmonics(): lax.all_to_all(payload, 'tm', split_axis=1, concat_axis=0, tiled=True)  183 us
    all_to_all x1, waiting for transfers between devices, to_harmonics(): lax.all_to_all(harmonic, 'tm', split_axis=0, concat_axis=1, tiled=True)  155 us
    scatter x1, local copies, waits for them, and re-layouts, to_owners(): buffer = buffer.at[:, slot_index, :].set(payload)  104 us
    all_to_all x1, blocking collectives, to_owners(): lax.all_to_all(buffer, ('sx', 'sy'), split_axis=1, concat_axis=1, tiled=T...  99.1 us
    ppermute x8, starting transfers between devices, with_halo(): lax.ppermute(lax.slice_in_dim(block, block.shape[dim] - width, None, axis...  33.2 us
    all_to_all x2, local copies, waits for them, and re-layouts, to_harmonics(): lax.all_to_all(harmonic, 'tm', split_axis=0, concat_axis=1, tiled=True)  28.9 us
    unnamed x53, local copies, waits for them, and re-layouts  22.3 us
    concatenate x6, other arithmetic, with_halo(): block = jnp.concatenate([low, block, high], axis=dim)  18.4 us
  transfers between devices with their start and end apart: 19, of which 15 were waited for; matrix products, arithmetic and copies ran while one was open for 4% of the time, Pallas kernels for 0%

commit v1 on v0

--- a/solution.py
+++ b/solution.py
@@ -1,8 +1,11 @@
+import functools
 import math
 
 import jax
 import jax.numpy as jnp
 from jax import lax
+from jax.experimental import pallas as pl
+from jax.experimental.pallas import tpu as pltpu
 from jax.sharding import PartitionSpec as P
 
 TIME = 64
@@ -128,6 +131,315 @@
     return field
 
 
+RADIX = 4
+GROUP = 2
+
+
+def zero_refs(cond, refs):
+    @pl.when(cond)
+    def _():
+        for ref in refs:
+            ref[...] = jnp.zeros(ref.shape, ref.dtype)
+
+
+def relax_kernel(
+    counts, cond_ref, cap_ref, cos_ref, sin_ref, mat_ref, rows_ref, out_ref,
+    conduct, heat, cy_send, cx_recv, cy_recv, coef, real_den, part_a, part_b, source,
+    field_a, field_b, x_send, x_recv, y_send, y_recv,
+    c_ssem, c_rsem, x_ssem, x_rsem, y_ssem, y_rsem,
+):
+    size_x, size_y, size_z = mat_ref.shape
+    harms = source.shape[0]
+    groups = harms // GROUP
+    place = {axis: lax.axis_index(axis) for axis in ("sx", "sy")}
+    has = {
+        axis: (place[axis] > 0, place[axis] < counts[axis] - 1) for axis in ("sx", "sy")
+    }
+    beside = {axis: (place[axis] - 1, place[axis] + 1) for axis in ("sx", "sy")}
+    sides = [(axis, side) for axis in ("sx", "sy") for side in (0, 1)]
+
+    barrier = pltpu.get_barrier_semaphore()
+    expected = jnp.int32(0)
+    for axis, side in sides:
+        expected = expected + has[axis][side].astype(jnp.int32)
+
+        @pl.when(has[axis][side])
+        def _(axis=axis, side=side):
+            pl.semaphore_signal(
+                barrier, inc=1, device_id={axis: beside[axis][side]},
+                device_id_type=pl.DeviceIdType.MESH,
+            )
+
+    for axis, (c_buf, f_buf) in {"sx": (cx_recv, x_recv), "sy": (cy_recv, y_recv)}.items():
+        for side in (0, 1):
+            zero_refs(
+                jnp.logical_not(has[axis][side]),
+                [c_buf.at[side]] + [f_buf.at[s, side] for s in range(SWEEPS - 1)],
+            )
+
+    def cell_values(x, carry):
+        mat = mat_ref[x]
+        con = jnp.zeros(mat.shape, jnp.float32)
+        cap = jnp.zeros(mat.shape, jnp.float32)
+        for m in range(NMAT):
+            con = jnp.where(mat == m, cond_ref[m], con)
+            cap = jnp.where(mat == m, cap_ref[m], cap)
+        conduct[x] = con
+        heat[x] = cap
+        cy_send[0, pl.ds(x, 1), :] = con[0:1]
+        cy_send[1, pl.ds(x, 1), :] = con[size_y - 1 :]
+        return carry
+
+    lax.fori_loop(0, size_x, cell_values, 0)
+    pl.semaphore_wait(barrier, expected)
+
+    def c_copy(axis, side, toward):
+        if axis == "sx":
+            src, dst = conduct.at[(size_x - 1) * side], cx_recv.at[1 - side]
+        else:
+            src, dst = cy_send.at[side], cy_recv.at[1 - side]
+        slot = 0 if axis == "sx" else 1
+        return pltpu.make_async_remote_copy(
+            src_ref=src, dst_ref=dst, send_sem=c_ssem.at[slot, side],
+            recv_sem=c_rsem.at[slot, 1 - side],
+            device_id={axis: beside[axis][toward]}, device_id_type=pl.DeviceIdType.MESH,
+        )
+
+    def f_copy(s, g, axis, side, toward):
+        send, recv, ssem, rsem = (
+            (x_send, x_recv, x_ssem, x_rsem) if axis == "sx" else (y_send, y_recv, y_ssem, y_rsem)
+        )
+        part = pl.ds(g * GROUP, GROUP)
+        return pltpu.make_async_remote_copy(
+            src_ref=send.at[s, side, part], dst_ref=recv.at[s, 1 - side, part],
+            send_sem=ssem.at[s, g, side], recv_sem=rsem.at[s, g, 1 - side],
+            device_id={axis: beside[axis][toward]}, device_id_type=pl.DeviceIdType.MESH,
+        )
+
+    def each(fn):
+        for axis, side in sides:
+
+            @pl.when(has[axis][side])
+            def _(axis=axis, side=side):
+                fn(axis, side)
+
+    each(lambda axis, side: c_copy(axis, side, side).start())
+
+    quarter = rows_ref.shape[0] // RADIX
+
+    def transform(x, carry):
+        cells = pl.ds(pl.multiple_of(x * size_y, size_y), size_y)
+        real = [None] * harms
+        imag = [None] * harms
+        for b in range(quarter):
+            t0, t1, t2, t3 = [
+                rows_ref[a * quarter + b, cells, :].astype(jnp.float32) for a in range(RADIX)
+            ]
+            even, odd = t0 + t2, t1 + t3
+            turn_r, turn_i = t0 - t2, t3 - t1
+            folded = ((even + odd, None), (turn_r, turn_i), (even - odd, None), (turn_r, -turn_i))
+            for j in range(harms):
+                c, n = cos_ref[j * quarter + b], sin_ref[j * quarter + b]
+                fr, fi = folded[j % RADIX]
+                if fi is None:
+                    re, im = c * fr, n * fr
+                else:
+                    re, im = c * fr - n * fi, c * fi + n * fr
+                real[j] = re if b == 0 else real[j] + re
+                imag[j] = im if b == 0 else imag[j] + im
+        for j in range(harms):
+            source[j, 0, x] = real[j]
+            source[j, 1, x] = imag[j]
+        return carry
+
+    lax.fori_loop(0, size_x, transform, 0)
+
+    each(lambda axis, side: c_copy(axis, 1 - side, side).wait_recv())
+
+    first = (lax.axis_index("tm") * harms).astype(jnp.float32)
+    row = lax.broadcasted_iota(jnp.int32, (size_y, size_z), 0)
+    lane = lax.broadcasted_iota(jnp.int32, (size_y, size_z), 1)
+
+    def shift_y(value, low, high):
+        up = jnp.where(row == size_y - 1, high, pltpu.roll(value, size_y - 1, 0))
+        down = jnp.where(row == 0, low, pltpu.roll(value, 1, 0))
+        return up, down
+
+    def keep(s, h, x, real, imag, dst, pad):
+        for r, value in enumerate((real, imag)):
+            dst[h, r, x + pad] = value
+            if s < SWEEPS - 1:
+                y_send[s, 0, h, r, pl.ds(x, 1), :] = value[0:1]
+                y_send[s, 1, h, r, pl.ds(x, 1), :] = value[size_y - 1 :]
+
+    def prepare(x, carry):
+        own = conduct[x]
+        above = jnp.where(x == size_x - 1, cx_recv[1], conduct[jnp.minimum(x + 1, size_x - 1)])
+        below = jnp.where(x == 0, cx_recv[0], conduct[jnp.maximum(x - 1, 0)])
+        up, down = shift_y(own, cy_recv[0, pl.ds(x, 1), :], cy_recv[1, pl.ds(x, 1), :])
+        right = jnp.where(lane == size_z - 1, own, pltpu.roll(own, size_z - 1, 1))
+        left = jnp.where(lane == 0, own, pltpu.roll(own, 1, 1))
+        total = None
+        for i, other in enumerate((above, below, up, down, right, left)):
+            face = face_value(own, other)
+            total = face if total is None else total + face
+            if i == 4:
+                face = jnp.where(lane == size_z - 1, 0.0, face)
+            if i == 5:
+                face = jnp.where(lane == 0, 0.0, face)
+            coef[i, x] = face
+        cap = heat[x]
+        for h in range(harms):
+            imag_den = (omega_step * (first + h)) * cap
+            inverse = 1.0 / (total * total + imag_den * imag_den)
+            a, b = total * inverse, imag_den * inverse
+            part_a[h, x] = a
+            part_b[h, x] = b
+            sr, si = source[h, 0, x], source[h, 1, x]
+            keep(0, h, x, sr * a + si * b, si * a - sr * b, field_a, 1)
+        return carry
+
+    lax.fori_loop(0, size_x, prepare, 0)
+
+    def send_group(s, g, field):
+        for j in range(GROUP):
+            h = g * GROUP + j
+            for r in range(2):
+                x_send[s, 0, h, r] = field[h, r, 1].astype(x_send.dtype)
+                x_send[s, 1, h, r] = field[h, r, size_x].astype(x_send.dtype)
+        each(lambda axis, side: f_copy(s, g, axis, side, side).start())
+
+    def launch(g, carry):
+        send_group(0, g, field_a)
+        return carry
+
+    lax.fori_loop(0, groups, launch, 0)
+
+    for s in range(1, SWEEPS):
+        old = field_a if s % 2 == 1 else field_b
+        last = s == SWEEPS - 1
+        new = out_ref if last else (field_b if s % 2 == 1 else field_a)
+        pad = 0 if last else 1
+
+        def sweep(g, carry, s=s, old=old, new=new, pad=pad, last=last):
+            each(lambda axis, side: f_copy(s - 1, g, axis, 1 - side, side).wait_recv())
+            for j in range(GROUP):
+                h = g * GROUP + j
+                for r in range(2):
+                    old[h, r, 0] = x_recv[s - 1, 0, h, r].astype(jnp.float32)
+                    old[h, r, size_x + 1] = x_recv[s - 1, 1, h, r].astype(jnp.float32)
+
+            def plane(x, inner):
+                faces = [coef[i, x] for i in range(6)]
+                for j in range(GROUP):
+                    h = g * GROUP + j
+                    nums = []
+                    for r in range(2):
+                        own = old[h, r, x + 1]
+                        up, down = shift_y(
+                            own,
+                            y_recv[s - 1, 0, h, r, pl.ds(x, 1), :],
+                            y_recv[s - 1, 1, h, r, pl.ds(x, 1), :],
+                        )
+                        num = source[h, r, x] + faces[0] * old[h, r, x + 2]
+                        num = num + faces[1] * old[h, r, x]
+                        num = num + (faces[2] * up + faces[3] * down)
+                        num = num + faces[4] * pltpu.roll(own, size_z - 1, 1)
+                        num = num + faces[5] * pltpu.roll(own, 1, 1)
+                        nums.append(num)
+                    a, b = part_a[h, x], part_b[h, x]
+                    keep(
+                        s, h, x, nums[0] * a + nums[1] * b, nums[1] * a - nums[0] * b, new, pad
+                    )
+                return inner
+
+            lax.fori_loop(0, size_x, plane, 0)
+            if not last:
+                send_group(s, g, new)
+            return carry
+
+        lax.fori_loop(0, groups, sweep, 0)
+
+    each(lambda axis, side: c_copy(axis, side, side).wait_send())
+
+    def finish(g, carry):
+        for s in range(SWEEPS - 1):
+            each(lambda axis, side, s=s: f_copy(s, g, axis, side, side).wait_send())
+        return carry
+
+    lax.fori_loop(0, groups, finish, 0)
+
+
+def relax(rows, material, conductivity, capacity):
+    size_x, size_y, size_z = material.shape
+    harms = HARM // lax.axis_size("tm")
+    groups = harms // GROUP
+    quarter = TIME // RADIX
+    table = dft_table().astype(jnp.float32).reshape(HARM, 2, TIME)[:, :, :quarter]
+    table = lax.dynamic_slice_in_dim(table, lax.axis_index("tm") * harms, harms, 0)
+    f32, bf16 = jnp.float32, jnp.bfloat16
+    tile = (size_x, size_y, size_z)
+    padded = (harms, 2, size_x + 2, size_y, size_z)
+    x_edge = (SWEEPS - 1, 2, harms, 2, size_y, size_z)
+    y_edge = (SWEEPS - 1, 2, harms, 2, size_x, size_z)
+    dma = pltpu.SemaphoreType.DMA
+    counts = {axis: lax.axis_size(axis) for axis in ("sx", "sy")}
+    smem = pl.BlockSpec(memory_space=pltpu.SMEM)
+    vmem = pl.BlockSpec(memory_space=pltpu.VMEM)
+    return pl.pallas_call(
+        functools.partial(relax_kernel, counts),
+        out_shape=jax.ShapeDtypeStruct((harms, 2) + tile, f32),
+        in_specs=[smem] * 4 + [vmem] * 2,
+        out_specs=vmem,
+        scratch_shapes=[
+            pltpu.VMEM(tile, f32),
+            pltpu.VMEM(tile, f32),
+            pltpu.VMEM((2, size_x, size_z), f32),
+            pltpu.VMEM((2, size_y, size_z), f32),
+            pltpu.VMEM((2, size_x, size_z), f32),
+            pltpu.VMEM((6,) + tile, f32),
+            pltpu.VMEM(tile, f32),
+            pltpu.VMEM((harms,) + tile, f32),
+            pltpu.VMEM((harms,) + tile, f32),
+            pltpu.VMEM((harms, 2) + tile, f32),
+            pltpu.VMEM(padded, f32),
+            pltpu.VMEM(padded, f32),
+            pltpu.VMEM(x_edge, bf16),
+            pltpu.VMEM(x_edge, bf16),
+            pltpu.VMEM(y_edge, f32),
+            pltpu.VMEM(y_edge, f32),
+            dma((2, 2)),
+            dma((2, 2)),
+            dma((SWEEPS - 1, groups, 2)),
+            dma((SWEEPS - 1, groups, 2)),
+            dma((SWEEPS - 1, groups, 2)),
+            dma((SWEEPS - 1, groups, 2)),
+        ],
+        compiler_params=pltpu.CompilerParams(
+            collective_id=1, has_side_effects=True, vmem_limit_bytes=48 * 1024 * 1024
+        ),
+    )(
+        conductivity,
+        capacity,
+        table[:, 0].reshape(-1),
+        table[:, 1].reshape(-1),
+        material,
+        rows,
+    )
+
+
+def fast_body(wall_temp, owner_map, stencil_column, material, conductivity, capacity):
+    cells = material.shape[0] * material.shape[1]
+    total = cells * lax.axis_size("sx") * lax.axis_size("sy")
+    target = owner_map[:, 0] * cells + stencil_column
+    hits = (jnp.arange(total, dtype=jnp.int32)[:, None] == target[None, :]).astype(jnp.bfloat16)
+    summed = jnp.einsum("sp,tpz->tsz", hits, wall_temp, preferred_element_type=jnp.float32)
+    summed = summed.astype(jnp.bfloat16)
+    mine = lax.psum_scatter(summed, ("sx", "sy"), scatter_dimension=1, tiled=True)
+    rows = lax.all_gather(mine, "tm", axis=0, tiled=True)
+    return relax(rows, material, conductivity, capacity)
+
+
 def solution(mesh):
     in_specs = (
         P("tm", ("sx", "sy"), None),
@@ -138,4 +450,6 @@
         P(),
     )
     out_specs = P("tm", None, "sx", "sy", None)
-    return jax.shard_map(body, mesh=mesh, in_specs=in_specs, out_specs=out_specs, check_vma=False)
+    direct = mesh.shape["tm"] == RADIX and mesh.shape["sx"] == 2 and mesh.shape["sy"] == 4
+    step = fast_body if direct else body
+    return jax.shard_map(step, mesh=mesh, in_specs=in_specs, out_specs=out_specs, check_vma=False)

time: 760 us -> 218 us (0.29)
  waiting for transfers between devices: 351 us -> 156 us
  local copies, waits for them, and re-layouts: 172 us -> 1.49 us
  blocking collectives: 99.1 us -> 0 us
  starting transfers between devices: 66.5 us -> 0.04 us
  other arithmetic: 45 us -> 1.48 us
  Pallas kernels: 0 us -> 32.5 us
  between operations: 0.69 us -> 13.4 us
    all_to_all x3 -> x0, waiting for transfers between devices: 338 us -> none  [the longest x1 183 us: to_harmonics(): lax.all_to_all(payload, 'tm', split_axis=1, concat_axis=0, tiled=True)]
    scatter x1 -> x0, local copies, waits for them, and re-layouts: 104 us -> none  [to_owners(): buffer = buffer.at[:, slot_index, :].set(payload)]
    all_to_all x1 -> x0, blocking collectives: 99.1 us -> none  [to_owners(): lax.all_to_all(buffer, ('sx', 'sy'), split_axis=1, concat_axis=1, tiled=T...]
    all_gather x0 -> x1, waiting for transfers between devices: none -> 82.1 us  [fast_body(): rows = lax.all_gather(mine, 'tm', axis=0, tiled=True)]
    reduce_scatter x0 -> x1, waiting for transfers between devices: none -> 73.5 us  [fast_body(): lax.psum_scatter(summed, ('sx', 'sy'), scatter_dimension=1, tiled=True)]
    ppermute x16 -> x0, starting transfers between devices: 50.2 us -> none  [the longest x8 33.2 us: with_halo(): lax.ppermute(lax.slice_in_dim(block, block.shape[dim] - width, None, axis...]
    all_to_all x3 -> x0, local copies, waits for them, and re-layouts: 37.7 us -> none  [the longest x2 28.9 us: to_harmonics(): lax.all_to_all(harmonic, 'tm', split_axis=0, concat_axis=1, tiled=True)]
    pallas_call x0 -> x1, Pallas kernels: none -> 32.5 us  [relax(): pl.pallas_call(functools.partial(relax_kernel, counts), out_shape=jax.Sha...]
  transfers between devices with their start and end apart: 19 -> 2, of which waited for: 15 -> 2; matrix products, arithmetic and copies ran while one was open for 4% -> 0% of each run, Pallas kernels for 0% -> 0%
where the time goes in v1:
time: 218 us
  waiting for transfers between devices  156 us (72%)
  Pallas kernels  32.5 us (15%)
  between operations  13.4 us (6%)
  matrix products  12.9 us (6%)
    all_gather x1, waiting for transfers between devices, fast_body(): rows = lax.all_gather(mine, 'tm', axis=0, tiled=True)  82.1 us
    reduce_scatter x1, waiting for transfers between devices, fast_body(): lax.psum_scatter(summed, ('sx', 'sy'), scatter_dimension=1, tiled=True)  73.5 us
    pallas_call x1, Pallas kernels, relax(): pl.pallas_call(functools.partial(relax_kernel, counts), out_shape=jax.Sha...  32.5 us
    dot_general x1, matrix products, fast_body(): jnp.einsum('sp,tpz->tsz', hits, wall_temp, preferred_element_type=jnp.flo...  12.9 us
  transfers between devices with their start and end apart: 2, of which 2 were waited for; matrix products, arithmetic and copies ran while one was open for 0% of the time, Pallas kernels for 0%

profile of v1, /device:TPU:1, one launch (start us, length us, event | category | flops | bytes accessed | tf_op | source)
XLA Modules:
  0.0 217.5 jit_solution(4498820894114122020)
XLA Ops:
  6.5 0.0 reduce-scatter.2.cloned.1.call-start
  6.5 0.7 broadcast_multiply_fusion
  7.2 0.7 add.29
  7.9 12.9 %convert_bitcast_fusion = bf16[16,2048,128]{2,1,0:T(8,128)(2,1)} fusion(bf16[16,1024,128]{2,1,0:T(8,128)(2,1)} %param.6, s32[1024]{0:T(1024)S(1)} %add.29), kind=kOutput, calls=%fused_computation | convolution fusion | flops 8596226048 | bytes 12587008 | tf_op jit(solution)/shard_map/sp,tpz->tsz/dot_general | solution.py:436
  20.9 0.0 copy-start
  20.9 0.0 copy-start.1
  20.9 0.0 copy-start.2
  20.9 0.0 reduce-scatter.2.cloned.1.call-update
  20.9 0.0 all-gather.2.cloned.1.call-start
  20.9 73.5 %reduce-scatter.2.cloned.1.call-done = bf16[16,256,128]{2,1,0:T(8,128)(2,1)} async-done(((bf16[16,2048,128]{2,1,0:T(8,128)(2,1)}), bf16[16,256,128]{2,1,0:T(8,128)(2,1)}) %reduce-scatter.2.cloned.1.call-update) | async-done | bytes 1048592 | tf_op jit(solution)/shard_map/reduce_scatter | solution.py:438
  94.4 0.0 all-gather.2.cloned.1.call-update
  94.4 0.1 multiply_convert_fusion
  94.6 0.1 reshape_squeeze.7.sin_ref
  94.6 0.1 reshape_squeeze.6.cos_ref
  94.7 82.1 %all-gather.2.cloned.1.call-done.rows_ref = bf16[64,256,128]{2,1,0:T(8,128)(2,1)} async-done(((bf16[16,256,128]{2,1,0:T(8,128)(2,1)}), bf16[64,256,128]{2,1,0:T(8,128)(2,1)}) %all-gather.2.cloned.1.call-update) | async-done | bytes 4194320 | tf_op jit(solution)/shard_map/all_gather | solution.py:439
  176.8 0.0 copy-done
  176.8 0.0 copy-done.1
  176.8 0.0 copy-done.2
  176.8 32.5 %shard_map.64 = f32[8,2,16,16,128]{4,3,2,1,0:T(8,128)S(1)} custom-call(f32[4]{0:T(128)S(1)} %copy-done.1, f32[4]{0:T(128)S(1)} %copy-done.2, f32[128]{0:T(128)S(1)} %reshape_squeeze.6.cos_ref, f32[128]{0:T(128)S(1)} %reshape_squeeze.7.sin_ref, s32[16,16,128]{2,1,0:T(8,128)S(1)} %copy-done, bf16[64,256,128]{2,1,0:T(8,128)(2,1)} %all-gather.2.cloned.1.call-done.rows_ref), custom_call_target="tpu_custom_call" | custom-call | tf_op jit(solution)/shard_map/pallas_call | solution.py:389
  209.3 1.3 copy.8
  (2 shorter events, 0.0 us)
Async XLA Ops:
  6.5 87.9 %reduce-scatter.2.cloned.1.call-start = ((), (), s32[]{:S(2)}) async-start(), calls=%async_computation.1 | async-start | bytes 9437184 | tf_op jit(solution)/shard_map/reduce_scatter | solution.py:438
  20.9 156.0 %copy-start = (s32[16,16,128]{2,1,0:T(8,128)S(1)}, s32[16,16,128]{2,1,0:T(8,128)}, u32[]{:S(2)}) copy-start(s32[16,16,128]{2,1,0:T(8,128)} %mat_ref.1) | copy-start | bytes 393220
  20.9 156.0 %copy-start.1 = (f32[4]{0:T(128)S(1)}, f32[4]{0:T(128)}, u32[]{:S(2)}) copy-start(f32[4]{0:T(128)} %cond_ref.1) | copy-start | bytes 52
  20.9 156.0 %copy-start.2 = (f32[4]{0:T(128)S(1)}, f32[4]{0:T(128)}, u32[]{:S(2)}) copy-start(f32[4]{0:T(128)} %cap_ref.1) | copy-start | bytes 52
  20.9 155.9 %all-gather.2.cloned.1.call-start = ((), (), s32[]{:S(2)}) async-start(), calls=%async_computation.2 | async-start | bytes 5242880 | tf_op jit(solution)/shard_map/all_gather | solution.py:439
Sparse Core Ops, SparseCore 0:
  21.0 73.3 reduce-scatter.1
  96.1 80.7 all-gather.1

commit v2 on v1

--- a/solution.py
+++ b/solution.py
@@ -142,33 +142,47 @@
             ref[...] = jnp.zeros(ref.shape, ref.dtype)
 
 
-def relax_kernel(
-    counts, cond_ref, cap_ref, cos_ref, sin_ref, mat_ref, rows_ref, out_ref,
-    conduct, heat, cy_send, cx_recv, cy_recv, coef, real_den, part_a, part_b, source,
+LAGS = (1, 3, 5, 7, 9, 11)
+FACES_AT = 3
+RING = 4
+
+
+def blade_kernel(
+    counts, cond_ref, cap_ref, cos_ref, sin_ref, target_ref, wall_ref, mat_ref, out_ref,
+    hits, core_own, core_send, core_recv, one_keep, one_send, one_recv,
+    two_keep, two_send, two_recv, rows_ref,
+    conduct, heat, cy_send, cx_recv, cy_recv, coef, part_a, part_b, source,
     field_a, field_b, x_send, x_recv, y_send, y_recv,
+    core_ssem, core_rsem, one_ssem, one_rsem, two_ssem, two_rsem, z_ssem, z_rsem,
     c_ssem, c_rsem, x_ssem, x_rsem, y_ssem, y_rsem,
 ):
+    steps, patches, _ = wall_ref.shape
+    cells = rows_ref.shape[1]
     size_x, size_y, size_z = mat_ref.shape
     harms = source.shape[0]
     groups = harms // GROUP
-    place = {axis: lax.axis_index(axis) for axis in ("sx", "sy")}
-    has = {
-        axis: (place[axis] > 0, place[axis] < counts[axis] - 1) for axis in ("sx", "sy")
-    }
-    beside = {axis: (place[axis] - 1, place[axis] + 1) for axis in ("sx", "sy")}
+    tm, sx, sy = (lax.axis_index(axis) for axis in ("tm", "sx", "sy"))
+    x, core = sy // 2, sy % 2
+    mesh_id = pl.DeviceIdType.MESH
+    last = RADIX - 1
+    place = {"sx": sx, "sy": sy}
+    has = {axis: (place[axis] > 0, place[axis] < counts[axis] - 1) for axis in place}
+    beside = {axis: (place[axis] - 1, place[axis] + 1) for axis in place}
     sides = [(axis, side) for axis in ("sx", "sy") for side in (0, 1)]
+    inner = jnp.logical_and(has["sy"][0], has["sy"][1])
 
     barrier = pltpu.get_barrier_semaphore()
-    expected = jnp.int32(0)
-    for axis, side in sides:
-        expected = expected + has[axis][side].astype(jnp.int32)
-
-        @pl.when(has[axis][side])
-        def _(axis=axis, side=side):
-            pl.semaphore_signal(
-                barrier, inc=1, device_id={axis: beside[axis][side]},
-                device_id_type=pl.DeviceIdType.MESH,
-            )
+
+    def greet(*peer):
+        pl.semaphore_signal(barrier, inc=1, device_id=peer, device_id_type=mesh_id)
+
+    greet(tm, sx, 2 * x + 1 - core)
+    greet(tm, sx, 2 * (1 - x) + core)
+    greet(tm, 1 - sx, sy)
+    pl.when(tm > 0)(lambda: greet(tm - 1, sx, sy))
+    pl.when(tm < last)(lambda: greet(tm + 1, sx, sy))
+    pl.when(inner)(lambda: greet(tm, sx, 3 - sy))
+    expected = 3 + sum(flag.astype(jnp.int32) for flag in (tm > 0, tm < last, inner))
 
     for axis, (c_buf, f_buf) in {"sx": (cx_recv, x_recv), "sy": (cy_recv, y_recv)}.items():
         for side in (0, 1):
@@ -176,6 +190,16 @@
                 jnp.logical_not(has[axis][side]),
                 [c_buf.at[side]] + [f_buf.at[s, side] for s in range(SWEEPS - 1)],
             )
+
+    strip = 64
+
+    def mark(i, carry):
+        ids = lax.broadcasted_iota(jnp.int32, (strip, patches), 0) + i * strip
+        match = jnp.where(ids == target_ref[...], 1.0, 0.0)
+        hits[pl.ds(pl.multiple_of(i * strip, strip), strip), :] = match.astype(jnp.bfloat16)
+        return carry
+
+    lax.fori_loop(0, hits.shape[0] // strip, mark, 0)
 
     def cell_values(x, carry):
         mat = mat_ref[x]
@@ -191,7 +215,72 @@
         return carry
 
     lax.fori_loop(0, size_x, cell_values, 0)
+
+    def clear(h, carry):
+        for r in range(2):
+            source[h, r] = jnp.zeros((size_x, size_y, size_z), jnp.float32)
+        return carry
+
+    lax.fori_loop(0, harms, clear, 0)
     pl.semaphore_wait(barrier, expected)
+
+    def flip(bit, odd):
+        return bit + odd - 2 * bit * odd
+
+    def pick(c, u, v):
+        turn = c % 2
+        cell_x = flip(x, u + turn * (v - u))
+        cell_y = flip(sx, v + turn * (u - v))
+        return cell_y * 2 + cell_x
+
+    def core_copy(c):
+        return pltpu.make_async_remote_copy(
+            src_ref=core_send.at[c], dst_ref=core_recv.at[c],
+            send_sem=core_ssem.at[c], recv_sem=core_rsem.at[c],
+            device_id=(tm, sx, 2 * x + 1 - core), device_id_type=mesh_id,
+        )
+
+    def plane_copy(c, send, recv, ssem, rsem, along_y):
+        peer = (tm, flip(sx, along_y), 2 * flip(x, 1 - along_y) + core)
+        return pltpu.make_async_remote_copy(
+            src_ref=send.at[c], dst_ref=recv.at[c], send_sem=ssem.at[c], recv_sem=rsem.at[c],
+            device_id=peer, device_id_type=mesh_id,
+        )
+
+    def one_copy(c):
+        return plane_copy(c, one_send, one_recv, one_ssem, one_rsem, c % 2)
+
+    def two_copy(c):
+        return plane_copy(c, two_send, two_recv, two_ssem, two_rsem, 1 - c % 2)
+
+    def z_copy(c, down, block, hop, peer):
+        place = block * steps + c
+        return pltpu.make_async_remote_copy(
+            src_ref=rows_ref.at[place], dst_ref=rows_ref.at[place],
+            send_sem=z_ssem.at[down, hop, c], recv_sem=z_rsem.at[down, hop, c],
+            device_id=(peer, sx, sy), device_id_type=mesh_id,
+        )
+
+    def z_send(c, hop, act):
+        @pl.when(jnp.logical_and(tm < last, tm - hop >= 0))
+        def _():
+            act(z_copy(c, 0, tm - hop, hop, tm + 1))
+
+        @pl.when(jnp.logical_and(tm > 0, tm + hop <= last))
+        def _():
+            act(z_copy(c, 1, tm + hop, hop, tm - 1))
+
+    def z_arrive(c, hop):
+        @pl.when(tm - hop - 1 >= 0)
+        def _():
+            z_copy(c, 0, tm - hop - 1, hop, tm - 1).wait_recv()
+
+        @pl.when(tm + hop + 1 <= last)
+        def _():
+            z_copy(c, 1, tm + hop + 1, hop, tm + 1).wait_recv()
+
+    def start(copy):
+        copy.start()
 
     def c_copy(axis, side, toward):
         if axis == "sx":
@@ -225,37 +314,6 @@
 
     each(lambda axis, side: c_copy(axis, side, side).start())
 
-    quarter = rows_ref.shape[0] // RADIX
-
-    def transform(x, carry):
-        cells = pl.ds(pl.multiple_of(x * size_y, size_y), size_y)
-        real = [None] * harms
-        imag = [None] * harms
-        for b in range(quarter):
-            t0, t1, t2, t3 = [
-                rows_ref[a * quarter + b, cells, :].astype(jnp.float32) for a in range(RADIX)
-            ]
-            even, odd = t0 + t2, t1 + t3
-            turn_r, turn_i = t0 - t2, t3 - t1
-            folded = ((even + odd, None), (turn_r, turn_i), (even - odd, None), (turn_r, -turn_i))
-            for j in range(harms):
-                c, n = cos_ref[j * quarter + b], sin_ref[j * quarter + b]
-                fr, fi = folded[j % RADIX]
-                if fi is None:
-                    re, im = c * fr, n * fr
-                else:
-                    re, im = c * fr - n * fi, c * fi + n * fr
-                real[j] = re if b == 0 else real[j] + re
-                imag[j] = im if b == 0 else imag[j] + im
-        for j in range(harms):
-            source[j, 0, x] = real[j]
-            source[j, 1, x] = imag[j]
-        return carry
-
-    lax.fori_loop(0, size_x, transform, 0)
-
-    each(lambda axis, side: c_copy(axis, 1 - side, side).wait_recv())
-
     first = (lax.axis_index("tm") * harms).astype(jnp.float32)
     row = lax.broadcasted_iota(jnp.int32, (size_y, size_z), 0)
     lane = lax.broadcasted_iota(jnp.int32, (size_y, size_z), 1)
@@ -272,7 +330,7 @@
                 y_send[s, 0, h, r, pl.ds(x, 1), :] = value[0:1]
                 y_send[s, 1, h, r, pl.ds(x, 1), :] = value[size_y - 1 :]
 
-    def prepare(x, carry):
+    def set_faces(x, carry):
         own = conduct[x]
         above = jnp.where(x == size_x - 1, cx_recv[1], conduct[jnp.minimum(x + 1, size_x - 1)])
         below = jnp.where(x == 0, cx_recv[0], conduct[jnp.maximum(x - 1, 0)])
@@ -295,6 +353,117 @@
             a, b = total * inverse, imag_den * inverse
             part_a[h, x] = a
             part_b[h, x] = b
+        return carry
+
+    def for_partner(c):
+        pair = jnp.concatenate([wall_ref[c], wall_ref[c + 1]], axis=1)
+
+        def sums(own_core):
+            rows = pl.ds(pl.multiple_of(own_core * (4 * cells), 4 * cells), 4 * cells)
+            return jnp.dot(hits[rows, :], pair, preferred_element_type=jnp.float32)
+
+        sent = sums(1 - core).astype(jnp.bfloat16)
+        for n in range(2):
+            core_send[c + n] = sent[:, n * size_z : (n + 1) * size_z].reshape(4, cells, size_z)
+            core_copy(c + n).start()
+        kept = sums(core)
+        for n in range(2):
+            core_own[(c + n) % RING] = kept[:, n * size_z : (n + 1) * size_z].reshape(
+                4, cells, size_z
+            )
+
+    def first_turn(c):
+        core_copy(c).wait_recv()
+        for u in (1, 0):
+            for v in range(2):
+                tile = pick(c, u, v)
+                both = core_own[c % RING, tile] + core_recv[c, tile].astype(jnp.float32)
+                if u == 1:
+                    one_send[c, v] = both.astype(jnp.bfloat16)
+                else:
+                    one_keep[c % RING, v] = both
+            if u == 1:
+                one_copy(c).start()
+
+    def second_turn(c):
+        one_copy(c).wait_recv()
+        two_send[c] = (one_keep[c % RING, 1] + one_recv[c, 1].astype(jnp.float32)).astype(
+            jnp.bfloat16
+        )
+        two_copy(c).start()
+        two_keep[c % RING] = one_keep[c % RING, 0] + one_recv[c, 0].astype(jnp.float32)
+
+    def complete(c):
+        two_copy(c).wait_recv()
+        total = two_keep[c % RING] + two_recv[c].astype(jnp.float32)
+        rows_ref[tm * steps + c] = total.astype(jnp.bfloat16)
+        z_send(c, 0, start)
+
+    def hop_one(c):
+        z_arrive(c, 0)
+        z_send(c, 1, start)
+
+    def hop_two(c):
+        z_arrive(c, 1)
+        z_send(c, 2, start)
+
+    def transform(c):
+        def plane(x, carry):
+            span = pl.ds(pl.multiple_of(x * size_y, size_y), size_y)
+            folded = []
+            for b in (c - 1, c):
+                t0, t1, t2, t3 = [
+                    rows_ref[a * steps + b, span, :].astype(jnp.float32) for a in range(RADIX)
+                ]
+                even, odd = t0 + t2, t1 + t3
+                turn_r, turn_i = t0 - t2, t3 - t1
+                folded.append(
+                    ((even + odd, None), (turn_r, turn_i), (even - odd, None), (turn_r, -turn_i))
+                )
+            for j in range(harms):
+                real, imag = source[j, 0, x], source[j, 1, x]
+                for n, b in enumerate((c - 1, c)):
+                    co, si = cos_ref[j * steps + b], sin_ref[j * steps + b]
+                    fr, fi = folded[n][j % RADIX]
+                    real = real + co * fr
+                    imag = imag + si * fr
+                    if fi is not None:
+                        real = real - si * fi
+                        imag = imag + co * fi
+                source[j, 0, x] = real
+                source[j, 1, x] = imag
+            return carry
+
+        lax.fori_loop(0, size_x, plane, 0)
+
+    def hop_three(c):
+        z_arrive(c, 2)
+        pl.when(c % 2 == 1)(lambda: transform(c))
+
+    stages = (first_turn, second_turn, complete, hop_one, hop_two, hop_three)
+
+    def at(i, lag, stage):
+        live = jnp.logical_and(i >= lag, i < steps + lag)
+        pl.when(live)(lambda: stage(i - lag))
+
+    def tick(i, carry):
+        for lag, stage in reversed(list(zip(LAGS[:-1], stages[:-1]))):
+            at(i, lag, stage)
+        pl.when(jnp.logical_and(i % 2 == 0, i < steps))(lambda: for_partner(i))
+
+        @pl.when(i == FACES_AT)
+        def _():
+            each(lambda axis, side: c_copy(axis, 1 - side, side).wait_recv())
+            lax.fori_loop(0, size_x, set_faces, 0)
+
+        at(i, LAGS[-1], hop_three)
+        return carry
+
+    lax.fori_loop(0, steps + LAGS[-1], tick, 0)
+
+    def prepare(x, carry):
+        for h in range(harms):
+            a, b = part_a[h, x], part_b[h, x]
             sr, si = source[h, 0, x], source[h, 1, x]
             keep(0, h, x, sr * a + si * b, si * a - sr * b, field_a, 1)
         return carry
@@ -317,11 +486,11 @@
 
     for s in range(1, SWEEPS):
         old = field_a if s % 2 == 1 else field_b
-        last = s == SWEEPS - 1
-        new = out_ref if last else (field_b if s % 2 == 1 else field_a)
-        pad = 0 if last else 1
-
-        def sweep(g, carry, s=s, old=old, new=new, pad=pad, last=last):
+        final = s == SWEEPS - 1
+        new = out_ref if final else (field_b if s % 2 == 1 else field_a)
+        pad = 0 if final else 1
+
+        def sweep(g, carry, s=s, old=old, new=new, pad=pad, final=final):
             each(lambda axis, side: f_copy(s - 1, g, axis, 1 - side, side).wait_recv())
             for j in range(GROUP):
                 h = g * GROUP + j
@@ -354,7 +523,7 @@
                 return inner
 
             lax.fori_loop(0, size_x, plane, 0)
-            if not last:
+            if not final:
                 send_group(s, g, new)
             return carry
 
@@ -369,75 +538,90 @@
 
     lax.fori_loop(0, groups, finish, 0)
 
-
-def relax(rows, material, conductivity, capacity):
+    def drain(c, carry):
+        core_copy(c).wait_send()
+        one_copy(c).wait_send()
+        two_copy(c).wait_send()
+        for hop in range(RADIX - 1):
+            z_send(c, hop, lambda copy: copy.wait_send())
+        return carry
+
+    lax.fori_loop(0, steps, drain, 0)
+
+
+def fast_body(wall_temp, owner_map, stencil_column, material, conductivity, capacity):
+    steps, patches, _ = wall_temp.shape
     size_x, size_y, size_z = material.shape
+    cells = size_x * size_y
+    total = cells * lax.axis_size("sx") * lax.axis_size("sy")
+    owner = owner_map[:, 0]
+    target = ((owner % 2) * (total // 2) + (owner // 2) * cells + stencil_column)[None, :]
     harms = HARM // lax.axis_size("tm")
     groups = harms // GROUP
-    quarter = TIME // RADIX
-    table = dft_table().astype(jnp.float32).reshape(HARM, 2, TIME)[:, :, :quarter]
+    table = dft_table().astype(jnp.float32).reshape(HARM, 2, TIME)[:, :, :steps]
     table = lax.dynamic_slice_in_dim(table, lax.axis_index("tm") * harms, harms, 0)
     f32, bf16 = jnp.float32, jnp.bfloat16
     tile = (size_x, size_y, size_z)
+    flat = (cells, size_z)
     padded = (harms, 2, size_x + 2, size_y, size_z)
     x_edge = (SWEEPS - 1, 2, harms, 2, size_y, size_z)
     y_edge = (SWEEPS - 1, 2, harms, 2, size_x, size_z)
-    dma = pltpu.SemaphoreType.DMA
+    shapes = [
+        ((total, patches), bf16),
+        ((RING, 4) + flat, f32),
+        ((steps, 4) + flat, bf16),
+        ((steps, 4) + flat, bf16),
+        ((RING, 2) + flat, f32),
+        ((steps, 2) + flat, bf16),
+        ((steps, 2) + flat, bf16),
+        ((RING,) + flat, f32),
+        ((steps,) + flat, bf16),
+        ((steps,) + flat, bf16),
+        ((RADIX * steps,) + flat, bf16),
+        (tile, f32),
+        (tile, f32),
+        ((2, size_x, size_z), f32),
+        ((2, size_y, size_z), f32),
+        ((2, size_x, size_z), f32),
+        ((6,) + tile, f32),
+        ((harms,) + tile, f32),
+        ((harms,) + tile, f32),
+        ((harms, 2) + tile, f32),
+        (padded, f32),
+        (padded, f32),
+        (x_edge, bf16),
+        (x_edge, bf16),
+        (y_edge, f32),
+        (y_edge, f32),
+    ]
+    sems = (
+        [(steps,)] * 6
+        + [(2, RADIX - 1, steps)] * 2
+        + [(2, 2)] * 2
+        + [(SWEEPS - 1, groups, 2)] * 4
+    )
     counts = {axis: lax.axis_size(axis) for axis in ("sx", "sy")}
     smem = pl.BlockSpec(memory_space=pltpu.SMEM)
     vmem = pl.BlockSpec(memory_space=pltpu.VMEM)
     return pl.pallas_call(
-        functools.partial(relax_kernel, counts),
+        functools.partial(blade_kernel, counts),
         out_shape=jax.ShapeDtypeStruct((harms, 2) + tile, f32),
-        in_specs=[smem] * 4 + [vmem] * 2,
+        in_specs=[smem] * 4 + [vmem] * 3,
         out_specs=vmem,
-        scratch_shapes=[
-            pltpu.VMEM(tile, f32),
-            pltpu.VMEM(tile, f32),
-            pltpu.VMEM((2, size_x, size_z), f32),
-            pltpu.VMEM((2, size_y, size_z), f32),
-            pltpu.VMEM((2, size_x, size_z), f32),
-            pltpu.VMEM((6,) + tile, f32),
-            pltpu.VMEM(tile, f32),
-            pltpu.VMEM((harms,) + tile, f32),
-            pltpu.VMEM((harms,) + tile, f32),
-            pltpu.VMEM((harms, 2) + tile, f32),
-            pltpu.VMEM(padded, f32),
-            pltpu.VMEM(padded, f32),
-            pltpu.VMEM(x_edge, bf16),
-            pltpu.VMEM(x_edge, bf16),
-            pltpu.VMEM(y_edge, f32),
-            pltpu.VMEM(y_edge, f32),
-            dma((2, 2)),
-            dma((2, 2)),
-            dma((SWEEPS - 1, groups, 2)),
-            dma((SWEEPS - 1, groups, 2)),
-            dma((SWEEPS - 1, groups, 2)),
-            dma((SWEEPS - 1, groups, 2)),
-        ],
+        scratch_shapes=[pltpu.VMEM(*shape) for shape in shapes]
+        + [pltpu.SemaphoreType.DMA(shape) for shape in sems],
         compiler_params=pltpu.CompilerParams(
-            collective_id=1, has_side_effects=True, vmem_limit_bytes=48 * 1024 * 1024
+            collective_id=1, has_side_effects=True, vmem_limit_bytes=58 * 1024 * 1024
         ),
     )(
         conductivity,
         capacity,
         table[:, 0].reshape(-1),
         table[:, 1].reshape(-1),
+        target,
+        wall_temp,
         material,
-        rows,
     )
-
-
-def fast_body(wall_temp, owner_map, stencil_column, material, conductivity, capacity):
-    cells = material.shape[0] * material.shape[1]
-    total = cells * lax.axis_size("sx") * lax.axis_size("sy")
-    target = owner_map[:, 0] * cells + stencil_column
-    hits = (jnp.arange(total, dtype=jnp.int32)[:, None] == target[None, :]).astype(jnp.bfloat16)
-    summed = jnp.einsum("sp,tpz->tsz", hits, wall_temp, preferred_element_type=jnp.float32)
-    summed = summed.astype(jnp.bfloat16)
-    mine = lax.psum_scatter(summed, ("sx", "sy"), scatter_dimension=1, tiled=True)
-    rows = lax.all_gather(mine, "tm", axis=0, tiled=True)
-    return relax(rows, material, conductivity, capacity)
 
 
 def solution(mesh):

time: 218 us -> 121 us (0.56)
  waiting for transfers between devices: 156 us -> 0 us
  Pallas kernels: 32.5 us -> 115 us
  between operations: 13.4 us -> 0.03 us
  matrix products: 12.9 us -> 0 us
  local copies, waits for them, and re-layouts: 1.49 us -> 4.26 us
    pallas_call x1, Pallas kernels: 32.5 us -> 115 us  [fast_body(): pl.pallas_call(functools.partial(blade_kernel, counts), out_shape=jax.Sha...]
    all_gather x1 -> x0, waiting for transfers between devices: 82.1 us -> none  [fast_body(): rows = lax.all_gather(mine, 'tm', axis=0, tiled=True)]
    reduce_scatter x1 -> x0, waiting for transfers between devices: 73.5 us -> none  [fast_body(): lax.psum_scatter(summed, ('sx', 'sy'), scatter_dimension=1, tiled=True)]
    dot_general x1 -> x0, matrix products: 12.9 us -> none  [fast_body(): jnp.einsum('sp,tpz->tsz', hits, wall_temp, preferred_element_type=jnp.flo...]
  transfers between devices with their start and end apart: 2 -> 0, of which waited for: 2 -> 0; matrix products, arithmetic and copies ran while one was open for 0% -> 0% of each run, Pallas kernels for 0% -> 0%
where the time goes in v2:
time: 121 us
  Pallas kernels  115 us (95%)
  local copies, waits for them, and re-layouts  4.26 us (4%)
  other arithmetic  1.41 us (1%)
    pallas_call x1, Pallas kernels, fast_body(): pl.pallas_call(functools.partial(blade_kernel, counts), out_shape=jax.Sha...  115 us
    unnamed x1, local copies, waits for them, and re-layouts  3.1 us

profile of v2, /device:TPU:1, one launch (start us, length us, event | category | flops | bytes accessed | tf_op | source)
XLA Modules:
  0.0 120.6 jit_solution(10913740822642649832)
XLA Ops:
  0.0 1.3 %fusion.8 = s32[1024]{0:T(1024)} fusion(s32[1024]{0:T(1024)} %param.8, s32[1024]{0:T(1024)} %bitcast.7), kind=kLoop, calls=%fused_computation.20 | loop fusion | flops 23552 | bytes 12288 | tf_op jit(solution)/shard_map/add | solution.py:558
  1.3 0.1 multiply_convert_fusion
  1.4 0.6 reshape_squeeze.7.sin_ref
  2.0 0.6 reshape_squeeze.6.cos_ref
  2.6 114.9 %shard_map.64 = f32[8,2,16,16,128]{4,3,2,1,0:T(8,128)} custom-call(f32[4]{0:T(128)} %cond_ref.1, f32[4]{0:T(128)} %cap_ref.1, f32[128]{0:T(128)} %reshape_squeeze.6.cos_ref, f32[128]{0:T(128)} %reshape_squeeze.7.sin_ref, s32[1,1024]{1,0:T(1,128)} %bitcast.6, bf16[16,1024,128]{2,1,0:T(8,128)(2,1)} %wall_ref.1, s32[16,16,128]{2,1,0:T(8,128)} %mat_ref.1), custom_call_target="tpu_custom_call" | custom-call | tf_op jit(solution)/shard_map/pallas_call | solution.py:606
  117.5 3.1 %copy.8 = f32[8,2,16,16,128]{4,3,2,1,0:T(8,128)} copy(f32[8,2,16,16,128]{4,3,2,1,0:T(8,128)} %shard_map.64) | data formatting | bytes 4194304
  (2 shorter events, 0.0 us)

commit v3 on v2

--- a/solution.py
+++ b/solution.py
@@ -135,6 +135,15 @@
 GROUP = 2
 
 
+def planes(count, body, width):
+    def block(i, carry):
+        for n in range(width):
+            body(i * width + n, 0)
+        return carry
+
+    lax.fori_loop(0, count // width, block, 0)
+
+
 def zero_refs(cond, refs):
     @pl.when(cond)
     def _():
@@ -142,8 +151,8 @@
             ref[...] = jnp.zeros(ref.shape, ref.dtype)
 
 
-LAGS = (1, 3, 5, 7, 9, 11)
-FACES_AT = 3
+LAGS = (2, 5, 8, 11, 14, 17)
+FACES_AT = 4
 RING = 4
 
 
@@ -434,7 +443,7 @@
                 source[j, 1, x] = imag
             return carry
 
-        lax.fori_loop(0, size_x, plane, 0)
+        planes(size_x, plane, 2)
 
     def hop_three(c):
         z_arrive(c, 2)
@@ -454,7 +463,7 @@
         @pl.when(i == FACES_AT)
         def _():
             each(lambda axis, side: c_copy(axis, 1 - side, side).wait_recv())
-            lax.fori_loop(0, size_x, set_faces, 0)
+            planes(size_x, set_faces, 2)
 
         at(i, LAGS[-1], hop_three)
         return carry
@@ -468,7 +477,7 @@
             keep(0, h, x, sr * a + si * b, si * a - sr * b, field_a, 1)
         return carry
 
-    lax.fori_loop(0, size_x, prepare, 0)
+    planes(size_x, prepare, 2)
 
     def send_group(s, g, field):
         for j in range(GROUP):
@@ -522,7 +531,7 @@
                     )
                 return inner
 
-            lax.fori_loop(0, size_x, plane, 0)
+            planes(size_x, plane, 4)
             if not final:
                 send_group(s, g, new)
             return carry

time: 121 us -> 117 us (0.967)
  Pallas kernels: 115 us -> 111 us
    pallas_call x1, Pallas kernels: 115 us -> 111 us  [fast_body(): pl.pallas_call(functools.partial(blade_kernel, counts), out_shape=jax.Sha...]
where the time goes in v3:
time: 117 us
  Pallas kernels  111 us (95%)
  local copies, waits for them, and re-layouts  4.26 us (4%)
  other arithmetic  1.41 us (1%)
    pallas_call x1, Pallas kernels, fast_body(): pl.pallas_call(functools.partial(blade_kernel, counts), out_shape=jax.Sha...  111 us
    unnamed x1, local copies, waits for them, and re-layouts  3.1 us

profile of v3, /device:TPU:1, one launch (start us, length us, event | category | flops | bytes accessed | tf_op | source)
XLA Modules:
  0.0 117.1 jit_solution(6265892603147183417)
XLA Ops:
  0.0 1.3 %fusion.8 = s32[1024]{0:T(1024)} fusion(s32[1024]{0:T(1024)} %param.8, s32[1024]{0:T(1024)} %bitcast.7), kind=kLoop, calls=%fused_computation.20 | loop fusion | flops 23552 | bytes 12288 | tf_op jit(solution)/shard_map/add | solution.py:567
  1.3 0.1 multiply_convert_fusion
  1.4 0.6 reshape_squeeze.7.sin_ref
  2.0 0.6 reshape_squeeze.6.cos_ref
  2.6 111.4 %shard_map.64 = f32[8,2,16,16,128]{4,3,2,1,0:T(8,128)} custom-call(f32[4]{0:T(128)} %cond_ref.1, f32[4]{0:T(128)} %cap_ref.1, f32[128]{0:T(128)} %reshape_squeeze.6.cos_ref, f32[128]{0:T(128)} %reshape_squeeze.7.sin_ref, s32[1,1024]{1,0:T(1,128)} %bitcast.6, bf16[16,1024,128]{2,1,0:T(8,128)(2,1)} %wall_ref.1, s32[16,16,128]{2,1,0:T(8,128)} %mat_ref.1), custom_call_target="tpu_custom_call" | custom-call | tf_op jit(solution)/shard_map/pallas_call | solution.py:615
  114.0 3.1 %copy.8 = f32[8,2,16,16,128]{4,3,2,1,0:T(8,128)} copy(f32[8,2,16,16,128]{4,3,2,1,0:T(8,128)} %shard_map.64) | data formatting | bytes 4194304
  (2 shorter events, 0.0 us)
